TPU v7x, 32 devices: a whole 2x2x4 slice. The times are simulated.
32 devices in a mesh: gx: 8 (over z, y), yz: 4 (over x, core).
Axes of the slice: x: 2, y: 2, z: 4, core: 2. Of those that a mesh axis runs over, the one named last changes fastest.
Arguments:
- mean_mix: float32 [131072], P(('gx', 'yz')), may hold values from 0.05 to 0.95
- segregation: float32 [131072], P(('gx', 'yz')), may hold values from 0.012 to 0.3
- dissipation: float32 [131072], P(('gx', 'yz')), may hold values from 0.04 to 0.4
- les_map: int32 [131072], P(('gx', 'yz')), may hold values from 0 to 255
- cond_state: float32 [10, 64, 8192], P(None, None, ('gx', 'yz')), may hold values from -6 to 6
- slot_cell: int32 [8192], P(('gx', 'yz')), may hold values from 0 to 8191, as said below
- adjacency: int32 [4, 8192], P(None, ('gx', 'yz')), may hold values from 0 to 383
- substeps: int32 [8192], P(('gx', 'yz')), may hold values from 1 to 8
- coupling: float32 [10, 10], replicated, may hold values from -2 to 2
Outputs:
- species: float32 [10, 131072], P(None, ('gx', 'yz'))
- cond_new: float32 [10, 64, 8192], P(None, None, ('gx', 'yz'))
Inputs may be any that keep to these rules, and one draw needn't show every extreme that they name: `slot_cell`: A permutation of the CMC cells. The 256 slots of each device hold exactly 16 cells of each of half of the tiles and none of the others; each tile's cells lie on half of the devices, exactly 16 on each.
All inputs are finite; a program needn't handle non-finite values.
Results may differ from a plain program's by a relative error of at most 0.00018.
Values sent between devices are 32-bit elements; how exact they have to be, the bound alone decides.
A program may use at most 64 MiB of HBM per device.

v0:
```python
import jax
import jax.numpy as jnp
from jax import lax
from jax.sharding import PartitionSpec as P

tau_face = 0.12
floor_mass = 0.25


def padded(cells, sides, width):
    for axis, dim in sides:
        count = lax.axis_size(axis)
        ends = count - 1
        head = lax.slice_in_dim(cells, 0, width, axis=dim)
        tail = lax.slice_in_dim(cells, cells.shape[dim] - width, cells.shape[dim], axis=dim)
        cells = jnp.concatenate(
            [
                lax.ppermute(tail, axis, [(i, (i + 1) % count) for i in range(ends)]),
                cells,
                lax.ppermute(head, axis, [((i + 1) % count, i) for i in range(ends)]),
            ],
            axis=dim,
        )
    return cells


def beta_weights(mean_mix, segregation, bins_count):
    centre = (jnp.arange(bins_count, dtype=jnp.float32) + 0.5) / bins_count
    shape_sum = 1.0 / segregation - 1.0
    shape_low = mean_mix * shape_sum
    shape_high = (1.0 - mean_mix) * shape_sum
    log_weight = (shape_low[None, :] - 1.0) * jnp.log(centre)[:, None] + (
        shape_high[None, :] - 1.0
    ) * jnp.log(1.0 - centre)[:, None]
    density = jnp.exp(log_weight)
    return density / jnp.sum(density, axis=0, keepdims=True)


def chemistry(start_state, cond_ratio, step_count, coupling):
    step_size = 1.0 / jnp.maximum(step_count, 1.0)
    loop_end = jnp.max(step_count).astype(jnp.int32)

    def advance(substep, cond_now):
        below_bin = jnp.concatenate([cond_now[:, :1], cond_now[:, :-1]], axis=1)
        above_bin = jnp.concatenate([cond_now[:, 1:], cond_now[:, -1:]], axis=1)
        spread = cond_ratio[None] * (above_bin - 2.0 * cond_now + below_bin)
        source = jnp.tanh(
            jnp.einsum("jk,kbs->jbs", coupling, cond_now, precision=lax.Precision.HIGHEST)
        )
        advanced = cond_now + step_size[None, None] * (spread + source)
        active = substep.astype(jnp.float32) < step_count
        return jnp.where(active[None, None], advanced, cond_now)

    return lax.fori_loop(0, loop_end, advance, start_state)


def pack_order(target_dev, groups, slot_cap):
    marks_onehot = (target_dev[:, None] == jnp.arange(groups, dtype=jnp.int32)[None, :]).astype(
        jnp.int32
    )
    earlier = jnp.cumsum(marks_onehot, axis=0) - marks_onehot
    position = jnp.sum(earlier * marks_onehot, axis=1)
    return target_dev * slot_cap + position


def cell_sums(moments, les_map, cells):
    rows_count, les_count = moments.shape
    block_len = min(1024, les_count)
    count_blocks = les_count // block_len
    moment_blocks = moments.reshape(rows_count, count_blocks, block_len).transpose(1, 0, 2)
    map_blocks = les_map.reshape(count_blocks, block_len)

    def add_block(running, packed):
        block_part, block_map = packed
        onehot = (block_map[None, :] == jnp.arange(cells, dtype=jnp.int32)[:, None]).astype(
            jnp.float32
        )
        return (
            running + jnp.einsum("rl,cl->rc", block_part, onehot, precision=lax.Precision.HIGHEST),
            None,
        )

    running, unused = lax.scan(
        add_block, jnp.zeros((rows_count, cells), jnp.float32), (moment_blocks, map_blocks)
    )
    return running


def trade_pair(values, extra):
    got_values, got_extra = (
        lax.all_to_all(values, ("gx", "yz"), split_axis=1, concat_axis=1, tiled=True),
        lax.all_to_all(extra, ("gx", "yz"), split_axis=1, concat_axis=1, tiled=True),
    )
    return (got_values, got_extra)


def trade_one(values):
    return lax.all_to_all(values, ("gx", "yz"), split_axis=1, concat_axis=1, tiled=True)


def shards(
    mean_mix,
    segregation,
    dissipation,
    les_map,
    cond_state,
    slot_cell,
    adjacency,
    substeps,
    coupling,
):
    n_scalar, n_bins, n_slots = cond_state.shape
    n_les = mean_mix.shape[0]
    devices = lax.axis_size("gx") * lax.axis_size("yz")
    slot_cap = 2 * n_slots // devices
    rim_cells = n_slots // 8
    flat_rows = n_scalar * n_bins
    buf_width = devices * slot_cap
    home_tile = slot_cell // n_slots
    local_cell = slot_cell % n_slots
    send_pos = pack_order(home_tile, devices, slot_cap)
    state_flat = cond_state.reshape(flat_rows, n_slots)
    state_buf = jnp.zeros((flat_rows, buf_width), jnp.float32).at[:, send_pos].set(state_flat)
    cell_info = jnp.stack([(local_cell + 1).astype(jnp.float32), substeps.astype(jnp.float32)])
    info_buf = (
        jnp.zeros((cell_info.shape[0], buf_width), jnp.float32).at[:, send_pos].set(cell_info)
    )
    got_state, got_info = trade_pair(state_buf, info_buf)
    filled = got_info[0] > 0.5
    cell_index = jnp.where(filled, got_info[0].astype(jnp.int32) - 1, n_slots)
    safe_index = jnp.minimum(cell_index, n_slots - 1)
    fill_mask = filled.astype(jnp.float32)[None, :]
    home_state = (
        jnp.zeros((flat_rows, n_slots), jnp.float32).at[:, cell_index].set(got_state, mode="drop")
    )
    weights = beta_weights(mean_mix, segregation, n_bins)
    moments = jnp.concatenate([weights, dissipation[None, :] * weights], axis=0)
    cell_totals = cell_sums(moments, les_map, n_slots)
    cond_ratio = cell_totals[n_bins:] / jnp.maximum(cell_totals[:n_bins], floor_mass)
    rim_state = home_state[:, :rim_cells].reshape(1, 1, flat_rows, rim_cells)
    beside_all = padded(rim_state, (("gx", 0), ("yz", 1)), 1)
    extended = jnp.concatenate(
        [home_state, beside_all[0, 1], beside_all[2, 1], beside_all[1, 0], beside_all[1, 2]], axis=1
    )
    neighbour_sum = jnp.zeros_like(home_state)
    for face in range(4):
        neighbour_sum = neighbour_sum + jnp.take(extended, adjacency[face], axis=1)
    moved_state = home_state + tau_face * (neighbour_sum - 4.0 * home_state)
    home_steps = jnp.zeros((n_slots,), jnp.float32).at[cell_index].set(got_info[1], mode="drop")
    new_home = chemistry(
        moved_state.reshape(n_scalar, n_bins, n_slots), cond_ratio, home_steps, coupling
    ).reshape(flat_rows, n_slots)
    reply_buf = jnp.take(new_home, safe_index, axis=1) * fill_mask
    back_buf = trade_one(reply_buf)
    cond_new = jnp.take(back_buf, send_pos, axis=1).reshape(n_scalar, n_bins, n_slots)
    new_cube = new_home.reshape(n_scalar, n_bins, n_slots)
    block_len = min(1024, n_les)
    count_blocks = n_les // block_len
    weight_blocks = weights.reshape(n_bins, count_blocks, block_len).transpose(1, 0, 2)
    map_blocks = les_map.reshape(count_blocks, block_len)

    def block_species(packed):
        block_weight, block_map = packed
        return jnp.sum(block_weight[None] * jnp.take(new_cube, block_map, axis=2), axis=1)

    per_block = lax.map(block_species, (weight_blocks, map_blocks))
    species = per_block.transpose(1, 0, 2).reshape(n_scalar, n_les)
    return (species, cond_new)


def solution(mesh):
    placed = (
        P(("gx", "yz")),
        P(("gx", "yz")),
        P(("gx", "yz")),
        P(("gx", "yz")),
        P(None, None, ("gx", "yz")),
        P(("gx", "yz")),
        P(None, ("gx", "yz")),
        P(("gx", "yz")),
        P(),
    )
    return jax.shard_map(
        shards,
        mesh=mesh,
        in_specs=placed,
        out_specs=(P(None, ("gx", "yz")), P(None, None, ("gx", "yz"))),
        check_vma=False,
    )
```

profile of v0, /device:TPU:0, one launch (start us, length us, event | category | flops | bytes accessed | tf_op | source)
XLA Modules:
  0.0 258.7 jit_solution(4652502218391096535)
XLA Ops:
  5.2 7.3 %all-to-all-start = ((f32[2,32,16]{2,0,1:T(2,128)}), f32[2,32,16]{2,0,1:T(2,128)S(1)}, u32[]{:S(2)}, u32[]{:S(2)}) async-start(f32[2,32,16]{2,0,1:T(2,128)} %copy.49), calls=%async_computation | async-start | bytes 65536 | tf_op jit(solution)/shard_map/all_to_all | solution.py:92
  16.5 3.1 %while.33 = (s32[]{:T(128)}, f32[128,256]{1,0:T(8,128)S(1)}, f32[4,128,1024]{2,1,0:T(8,128)S(1)}, s32[4,1024]{1,0:T(4,128)S(1)}, s32[]{:T(128)}, /*index=5*/s32[]{:T(128)}) while((s32[]{:T(128)}, f32[128,256]{1,0:T(8,128)S(1)}, f32[4,128,1024]{2,1,0:T(8,128)S(1)}, s32[4,1024]{1,0:T(4,128)S(1)}, s32[]{:T(128)}, ...), condition=%wide.region_10.12_spmd.clone, body=%wide.region_9.11_spmd.clone.sunk | while | flops 402980864 | bytes 798807 | solution.py:83
  22.5 5.8 %all-to-all-start.1 = ((f32[640,32,16]{0,2,1:T(8,128)}), f32[640,32,16]{0,2,1:T(8,128)S(1)}, u32[]{:S(2)}, u32[]{:S(2)}) async-start(f32[640,32,16]{0,2,1:T(8,128)} %bitcast.16), calls=%async_computation.1 | async-start | bytes 2621440 | tf_op jit(solution)/shard_map/all_to_all | solution.py:91
  28.4 3.1 %exponential_divide_fusion = f32[4,64,1024]{1,2,0:T(8,128)} fusion(f32[4,1024]{1,0:T(4,128)S(1)} %div.58, f32[64]{0:T(128)S(1)} %get-tuple-element.212, f32[4,1024]{1,0:T(4,128)S(1)} %mul.144, f32[64]{0:T(128)S(1)} %get-tuple-element.213, f32[4,1024]{1,0:T(4,128)S(1)} %mul.139), kind=kLoop, calls=%fused_computation.37 | loop fusion | flops 1048576 | bytes 1098240 | tf_op jit(solution)/shard_map/div | solution.py:36
  35.8 24.7 %all-to-all-done.1 = f32[640,32,16]{0,2,1:T(8,128)S(1)} async-done(((f32[640,32,16]{0,2,1:T(8,128)}), f32[640,32,16]{0,2,1:T(8,128)S(1)}, u32[]{:S(2)}, u32[]{:S(2)}) %all-to-all-start.1) | async-done | bytes 1310752 | tf_op jit(solution)/shard_map/all_to_all | solution.py:91
  62.9 3.1 %collective-permute-start = (f32[1,1,640,32]{2,3,1,0:T(8,128)S(1)}, f32[1,1,640,32]{2,3,1,0:T(8,128)S(1)}, u32[]{:S(2)}, u32[]{:S(2)}) collective-permute-start(f32[1,1,640,32]{2,3,1,0:T(8,128)S(1)} %slice_bitcast_fusion.2), channel_id=1, source_target_pairs={{0,4},{4,8},{8,12},{12,16},{16,20},{20,24},{24,28},{1,5},{5,9},{9,... | collective-permute-start | bytes 245768 | tf_op jit(solution)/shard_map/ppermute | solution.py:18
  68.1 4.3 %collective-permute-done.1 = f32[1,1,640,32]{2,3,1,0:T(8,128)S(1)} collective-permute-done((f32[1,1,640,32]{2,3,1,0:T(8,128)S(1)}, f32[1,1,640,32]{2,3,1,0:T(8,128)S(1)}, u32[]{:S(2)}, u32[]{:S(2)}) %collective-permute-start.1) | collective-permute-done | bytes 81952 | tf_op jit(solution)/shard_map/ppermute | solution.py:20
  75.1 3.7 %collective-permute-done.3 = f32[3,1,640,32]{2,3,1,0:T(8,128)S(1)} collective-permute-done((f32[3,1,640,32]{2,3,1,0:T(8,128)S(1)}, f32[3,1,640,32]{2,3,1,0:T(8,128)S(1)}, u32[]{:S(2)}, u32[]{:S(2)}) %collective-permute-start.3) | collective-permute-done | bytes 245792 | tf_op jit(solution)/shard_map/ppermute | solution.py:20
  88.1 7.6 %while.31 = (s32[]{:T(128)}, f32[10,64,256]{2,0,1:T(8,128)}, s32[]{:T(128)}, f32[256]{0:T(256)S(1)}, f32[256]{0:T(256)S(1)}, /*index=5*/f32[64,256]{1,0:T(8,128)S(1)}, f32[10,10]{1,0:T(8,128)S(1)}, s32[]{:T(128)}) while((s32[]{:T(128)}, f32[10,64,256]{2,0,1:T(8,128)}, s32[]{:T(128)}, f32[256]{0:T(256)S(1)}, f32[256]{0:T(256)S(1)}, ...), condition=%wide.region_12.14_spmd, body=%wide.region_11.13_spmd.sunk | while | flops 21299460 | bytes 6622193 | solution.py:54
  97.3 2.7 %copy.55 = f32[10,64,256]{1,0,2:T(8,128)S(1)} copy(f32[10,64,256]{2,0,1:T(8,128)} %get-tuple-element.155) | data formatting | bytes 1310720 | tf_op jit(solution)/shard_map/while | solution.py:166
  100.2 2.6 gather_fusion.1
  102.8 2.7 %select_multiply_fusion = f32[640,32,16]{0,2,1:T(8,128)} fusion(f32[640,32,16]{0,2,1:T(8,128)} %bitcast.130, f32[32,16]{1,0:T(8,128)S(1)} %copy.60, pred[32,16]{1,0:T(8,128)(4,1)S(1)} %copy.57), kind=kLoop, calls=%fused_computation.38 | loop fusion | flops 655360 | bytes 2624000 | tf_op jit(solution)/shard_map/mul | solution.py:153
  105.5 27.7 %all-to-all-start.2 = ((f32[640,32,16]{0,2,1:T(8,128)}), f32[640,32,16]{0,2,1:T(8,128)}, u32[]{:S(2)}, u32[]{:S(2)}) async-start(f32[640,32,16]{0,2,1:T(8,128)} %select_multiply_fusion), calls=%async_computation.2 | async-start | bytes 2621440 | tf_op jit(solution)/shard_map/all_to_all | solution.py:98
  133.2 118.8 %while.32 = (s32[]{:T(128)}, f32[4,10,1024]{1,2,0:T(8,128)}, f32[4,64,1024]{1,2,0:T(8,128)}, s32[4,1024]{1,0:T(4,128)S(1)}, f32[10,64,256]{1,0,2:T(8,128)S(1)}, /*index=5*/s32[]{:T(128)}) while((s32[]{:T(128)}, f32[4,10,1024]{1,2,0:T(8,128)}, f32[4,64,1024]{1,2,0:T(8,128)}, s32[4,1024]{1,0:T(4,128)S(1)}, f32[10,64,256]{1,0,2:T(8,128)S(1)}, ...), condition=%wide.region_15.17_spmd, body=%wide.region_13.16_spmd.sunk | while | flops 1966082 | bytes 9288269 | solution.py:166
  133.3 10.6 %gather_fusion = f32[1024,10,64]{2,1,0:T(8,128)} fusion(f32[10,64,256]{1,0,2:T(8,128)S(1)} %get-tuple-element.392, s32[1024]{0:T(1024)S(1)} %broadcast_clamp_fusion.2), kind=kCustom, calls=%fused_computation.1.clone.1 | custom fusion | bytes 5246976 | tf_op jit(solution)/shard_map/while/body/eval_jaxpr/jit(_take)/gather | solution.py:164
  145.0 17.1 %fusion.45 = f32[10,1024]{0,1:T(8,128)S(1)} fusion(f32[1024,10,64]{2,1,0:T(8,128)} %gather_fusion, f32[64,1024]{0,1:T(8,128)S(1)} %dynamic-slice_bitcast_fusion.2, pred[1024]{0:T(1024)(128)(4,1)S(1)} %compare_and_fusion.8), kind=kLoop, calls=%fused_computation.21.clone.1 | loop fusion | flops 1955840 | bytes 2925568 | tf_op jit(solution)/shard_map/while/body/eval_jaxpr/reduce_sum | solution.py:164
  163.0 10.6 %gather_fusion = f32[1024,10,64]{2,1,0:T(8,128)} fusion(f32[10,64,256]{1,0,2:T(8,128)S(1)} %get-tuple-element.392, s32[1024]{0:T(1024)S(1)} %broadcast_clamp_fusion.2), kind=kCustom, calls=%fused_computation.1.clone.1 | custom fusion | bytes 5246976 | tf_op jit(solution)/shard_map/while/body/eval_jaxpr/jit(_take)/gather | solution.py:164
  174.7 17.1 %fusion.45 = f32[10,1024]{0,1:T(8,128)S(1)} fusion(f32[1024,10,64]{2,1,0:T(8,128)} %gather_fusion, f32[64,1024]{0,1:T(8,128)S(1)} %dynamic-slice_bitcast_fusion.2, pred[1024]{0:T(1024)(128)(4,1)S(1)} %compare_and_fusion.8), kind=kLoop, calls=%fused_computation.21.clone.1 | loop fusion | flops 1955840 | bytes 2925568 | tf_op jit(solution)/shard_map/while/body/eval_jaxpr/reduce_sum | solution.py:164
  192.7 10.6 %gather_fusion = f32[1024,10,64]{2,1,0:T(8,128)} fusion(f32[10,64,256]{1,0,2:T(8,128)S(1)} %get-tuple-element.392, s32[1024]{0:T(1024)S(1)} %broadcast_clamp_fusion.2), kind=kCustom, calls=%fused_computation.1.clone.1 | custom fusion | bytes 5246976 | tf_op jit(solution)/shard_map/while/body/eval_jaxpr/jit(_take)/gather | solution.py:164
  204.4 17.1 %fusion.45 = f32[10,1024]{0,1:T(8,128)S(1)} fusion(f32[1024,10,64]{2,1,0:T(8,128)} %gather_fusion, f32[64,1024]{0,1:T(8,128)S(1)} %dynamic-slice_bitcast_fusion.2, pred[1024]{0:T(1024)(128)(4,1)S(1)} %compare_and_fusion.8), kind=kLoop, calls=%fused_computation.21.clone.1 | loop fusion | flops 1955840 | bytes 2925568 | tf_op jit(solution)/shard_map/while/body/eval_jaxpr/reduce_sum | solution.py:164
  222.4 10.6 %gather_fusion = f32[1024,10,64]{2,1,0:T(8,128)} fusion(f32[10,64,256]{1,0,2:T(8,128)S(1)} %get-tuple-element.392, s32[1024]{0:T(1024)S(1)} %broadcast_clamp_fusion.2), kind=kCustom, calls=%fused_computation.1.clone.1 | custom fusion | bytes 5246976 | tf_op jit(solution)/shard_map/while/body/eval_jaxpr/jit(_take)/gather | solution.py:164
  234.1 17.1 %fusion.45 = f32[10,1024]{0,1:T(8,128)S(1)} fusion(f32[1024,10,64]{2,1,0:T(8,128)} %gather_fusion, f32[64,1024]{0,1:T(8,128)S(1)} %dynamic-slice_bitcast_fusion.2, pred[1024]{0:T(1024)(128)(4,1)S(1)} %compare_and_fusion.8), kind=kLoop, calls=%fused_computation.21.clone.1 | loop fusion | flops 1955840 | bytes 2925568 | tf_op jit(solution)/shard_map/while/body/eval_jaxpr/reduce_sum | solution.py:164
  252.0 2.9 %copy.62 = f32[10,4096]{1,0:T(8,128)} copy(f32[10,4096]{0,1:T(8,128)} %bitcast.35) | data formatting | bytes 327680 | tf_op jit(solution)/shard_map/reshape | solution.py:167
  255.0 2.6 %gather_fusion.2 = f32[256,640]{1,0:T(8,128)S(1)} fusion(f32[640,512]{0,1:T(8,128)} %bitcast.42, s32[1024]{0:T(1024)S(1)} %pad_clamp_fusion), kind=kCustom, calls=%fused_computation.6 | custom fusion | bytes 1311744 | tf_op jit(solution)/shard_map/jit(_take)/gather | solution.py:155
  (120 shorter events, 52.6 us)
Async XLA Ops:
  5.2 17.3 %all-to-all-start = ((f32[2,32,16]{2,0,1:T(2,128)}), f32[2,32,16]{2,0,1:T(2,128)S(1)}, u32[]{:S(2)}, u32[]{:S(2)}) async-start(f32[2,32,16]{2,0,1:T(2,128)} %copy.49), calls=%async_computation | async-start | bytes 65536 | tf_op jit(solution)/shard_map/all_to_all | solution.py:92
  16.5 3.2 %copy-start = (f32[10,64,256]{2,1,0:T(8,128)S(1)}, f32[10,64,256]{2,1,0:T(8,128)}, u32[]{:S(2)}) copy-start(f32[10,64,256]{2,1,0:T(8,128)} %param.21) | copy-start | bytes 1966084
  22.5 38.0 %all-to-all-start.1 = ((f32[640,32,16]{0,2,1:T(8,128)}), f32[640,32,16]{0,2,1:T(8,128)S(1)}, u32[]{:S(2)}, u32[]{:S(2)}) async-start(f32[640,32,16]{0,2,1:T(8,128)} %bitcast.16), calls=%async_computation.1 | async-start | bytes 2621440 | tf_op jit(solution)/shard_map/all_to_all | solution.py:91
  62.9 5.2 %collective-permute-start = (f32[1,1,640,32]{2,3,1,0:T(8,128)S(1)}, f32[1,1,640,32]{2,3,1,0:T(8,128)S(1)}, u32[]{:S(2)}, u32[]{:S(2)}) collective-permute-start(f32[1,1,640,32]{2,3,1,0:T(8,128)S(1)} %slice_bitcast_fusion.2), channel_id=1, source_target_pairs={{0,4},{4,8},{8,12},{12,16},{16,20},{20,24},{24,28},{1,5},{5,9},{9,... | collective-permute-start | bytes 245768 | tf_op jit(solution)/shard_map/ppermute | solution.py:18
  66.0 6.3 %collective-permute-start.1 = (f32[1,1,640,32]{2,3,1,0:T(8,128)S(1)}, f32[1,1,640,32]{2,3,1,0:T(8,128)S(1)}, u32[]{:S(2)}, u32[]{:S(2)}) collective-permute-start(f32[1,1,640,32]{2,3,1,0:T(8,128)S(1)} %slice_bitcast_fusion.2), channel_id=1, source_target_pairs={{4,0},{8,4},{12,8},{16,12},{20,16},{24,20},{28,24},{5,1},{9,5},{13... | collective-permute-start | bytes 245768 | tf_op jit(solution)/shard_map/ppermute | solution.py:20
  72.4 2.6 %collective-permute-start.2 = (f32[3,1,640,32]{2,3,1,0:T(8,128)S(1)}, f32[3,1,640,32]{2,3,1,0:T(8,128)S(1)}, u32[]{:S(2)}, u32[]{:S(2)}) collective-permute-start(f32[3,1,640,32]{2,3,1,0:T(8,128)S(1)} %pad_maximum_fusion), channel_id=1, source_target_pairs={{0,1},{1,2},{2,3},{4,5},{5,6},{6,7},{8,9},{9,10},{10,11},{12,13},{... | collective-permute-start | bytes 737288 | tf_op jit(solution)/shard_map/ppermute | solution.py:18
  73.7 5.1 %collective-permute-start.3 = (f32[3,1,640,32]{2,3,1,0:T(8,128)S(1)}, f32[3,1,640,32]{2,3,1,0:T(8,128)S(1)}, u32[]{:S(2)}, u32[]{:S(2)}) collective-permute-start(f32[3,1,640,32]{2,3,1,0:T(8,128)S(1)} %pad_maximum_fusion), channel_id=1, source_target_pairs={{1,0},{2,1},{3,2},{5,4},{6,5},{7,6},{9,8},{10,9},{11,10},{13,12},{... | collective-permute-start | bytes 737288 | tf_op jit(solution)/shard_map/ppermute | solution.py:20
  86.5 1.6 copy-start.1
  105.5 149.5 %all-to-all-start.2 = ((f32[640,32,16]{0,2,1:T(8,128)}), f32[640,32,16]{0,2,1:T(8,128)}, u32[]{:S(2)}, u32[]{:S(2)}) async-start(f32[640,32,16]{0,2,1:T(8,128)} %select_multiply_fusion), calls=%async_computation.2 | async-start | bytes 2621440 | tf_op jit(solution)/shard_map/all_to_all | solution.py:98
where the time goes:
time: 260 us; the launch traced here: 259 us
  local copies, waits for them, and re-layouts  86.7 us (33%)
  other arithmetic  81.3 us (31%)
  starting transfers between devices  47.9 us (18%)
  waiting for transfers between devices  33.4 us (13%)
  matrix products  7.47 us (3%)
    reduce_sum x4, other arithmetic, block_species(): jnp.sum(block_weight[None] * jnp.take(new_cube, block_map, axis=2), axis=1)  68.5 us
    gather x4, local copies, waits for them, and re-layouts, block_species(): jnp.take(new_cube, block_map, axis=2)  42.4 us
    all_to_all x1, starting transfers between devices, trade_one(): lax.all_to_all(values, ('gx', 'yz'), split_axis=1, concat_axis=1, tiled=T...  27.7 us
    all_to_all x1, waiting for transfers between devices, trade_pair(): lax.all_to_all(values, ('gx', 'yz'), split_axis=1, concat_axis=1, tiled=T...  24.7 us
    ppermute x2, waiting for transfers between devices, padded(): lax.ppermute(head, axis, [((i + 1) % count, i) for i in range(ends)])  8.04 us
    all_to_all x1, starting transfers between devices, trade_pair(): lax.all_to_all(extra, ('gx', 'yz'), split_axis=1, concat_axis=1, tiled=True)  7.3 us
    gather x4, local copies, waits for them, and re-layouts, shards(): neighbour_sum = neighbour_sum + jnp.take(extended, adjacency[face], axis=1)  6.02 us
    all_to_all x1, starting transfers between devices, trade_pair(): lax.all_to_all(values, ('gx', 'yz'), split_axis=1, concat_axis=1, tiled=T...  5.83 us
  transfers between devices with their start and end apart: 7, of which 4 were waited for; matrix products, arithmetic and copies ran while one was open for 53% of the time, Pallas kernels for 0%

commit v1 on v0

v1 whole, which is shorter than its diff:
```python
import functools

import jax
import jax.numpy as jnp
from jax import lax
from jax.experimental import pallas as pl
from jax.experimental.pallas import tpu as pltpu
from jax.sharding import PartitionSpec as P

tau_face = 0.12
floor_mass = 0.25
submax = 8
f32, bf16 = jnp.float32, jnp.bfloat16
NN = (((1,), (0,)), ((), ()))
NT = (((1,), (1,)), ((), ()))
TN = (((0,), (0,)), ((), ()))


def split(x):
    high = x.astype(bf16)
    low = (x - high.astype(f32)).astype(bf16)
    return high, low


def mm(a, b, dims):
    return lax.dot_general(a, b, dims, preferred_element_type=f32)


def iota(shape, dim):
    return lax.broadcasted_iota(jnp.int32, shape, dim)


def onehot(mask):
    return jnp.where(mask, 1.0, 0.0).astype(bf16)


def kernel(
    n_gx, n_yz, cap, chunk,
    mean_ref, seg_ref, diss_ref, map_ref, state_ref, slot_ref, adj_ref, steps_ref, coup_ref,
    species_ref, cond_ref,
    send, recv, reply, back, info_out, info_in, info_rows, halo_out, halo_in,
    weights, ratio, pack, unpack, q0, q1, new_high, new_low, step_row,
    s_send, s_recv, i_send, i_recv, b_send, b_recv, h_send, h_recv,
):
    n_scalar, n_bins, n_cells = state_ref.shape
    rows = n_scalar * n_bins
    n_les = mean_ref.shape[1]
    n = n_gx * n_yz
    slots = send.shape[0]
    capp = slots // n
    rim = halo_out.shape[0]
    gx, yz = lax.axis_index("gx"), lax.axis_index("yz")
    me = gx * n_yz + yz

    def coords(r):
        t = lax.rem(me + r, n)
        return t, (t // n_yz, lax.rem(t, n_yz))

    def block(ref, t):
        return ref.at[pl.ds(pl.multiple_of(t * capp, 8), capp)]

    def info_copy(r):
        t, dev = coords(r)
        return pltpu.make_async_remote_copy(
            info_out.at[t], info_in.at[me], i_send.at[r], i_recv.at[r],
            device_id=dev, device_id_type=pl.DeviceIdType.MESH)

    def state_copy(r):
        t, dev = coords(r)
        return pltpu.make_async_remote_copy(
            block(send, t), block(recv, me), s_send.at[r], s_recv.at[r],
            device_id=dev, device_id_type=pl.DeviceIdType.MESH)

    def back_copy(r):
        t, dev = coords(r)
        return pltpu.make_async_remote_copy(
            block(reply, t), block(back, me), b_send.at[r], b_recv.at[r],
            device_id=dev, device_id_type=pl.DeviceIdType.MESH)

    def each(body):
        def run(r, carry):
            body(r)
            return carry
        lax.fori_loop(1, n, run, 0)

    halo_in[...] = jnp.zeros_like(halo_in)
    barrier = pltpu.get_barrier_semaphore()

    def greet(r):
        _, dev = coords(r)
        pl.semaphore_signal(barrier, inc=1, device_id=dev, device_id_type=pl.DeviceIdType.MESH)

    each(greet)

    slot = slot_ref[...]
    home = slot // n_cells
    local = slot - home * n_cells
    marks = iota((n, n_cells), 0) == home
    before = onehot(iota((n_cells, n_cells), 0) < iota((n_cells, n_cells), 1))
    earlier = mm(onehot(marks), before, NN)
    marks_f = jnp.where(marks, 1.0, 0.0)
    position = jnp.sum(earlier * marks_f, axis=0, keepdims=True).astype(jnp.int32)
    send_pos = home * capp + position
    pack[...] = onehot(iota((slots, n_cells), 0) == send_pos)

    lane = iota((128, n_cells), 0)
    at_low = onehot(lane == position)
    at_high = onehot(lane - 64 == position)
    index_part = (marks_f * (local + 1).astype(f32)).astype(bf16)
    steps_part = (marks_f * steps_ref[...].astype(f32)).astype(bf16)
    info = mm(index_part, at_low, NT) + mm(steps_part, at_high, NT)
    for d in range(n):
        info_out[d] = info[d:d + 1, :]

    high, low = split(state_ref[...].reshape(rows, n_cells))
    send[...] = mm(pack[...], high, NT) + mm(pack[...], low, NT)

    pl.semaphore_wait(barrier, n - 1)
    each(lambda r: info_copy(r).start())
    each(lambda r: state_copy(r).start())
    info_in[pl.ds(me, 1)] = info_out[pl.ds(me, 1)]
    mine = pl.ds(pl.multiple_of(me * capp, 8), capp)
    recv[mine, :] = send[mine, :]

    centre = (iota((n_bins, 128), 0).astype(f32) + 0.5) / n_bins
    log_low = jnp.log(centre)[:, :1]
    log_high = jnp.log(1.0 - centre)[:, :1]
    ratio[...] = jnp.zeros_like(ratio)

    def les_part(i, carry):
        part = pl.ds(pl.multiple_of(i * chunk, chunk), chunk)
        mean = mean_ref[:, part]
        shape_sum = 1.0 / seg_ref[:, part] - 1.0
        shape_low = mean * shape_sum
        shape_high = (1.0 - mean) * shape_sum
        density = jnp.exp((shape_low - 1.0) * log_low + (shape_high - 1.0) * log_high)
        w = density / jnp.sum(density, axis=0, keepdims=True)
        weights[:, part] = w
        moments = jnp.concatenate([w, diss_ref[:, part] * w], axis=0)
        m_high, m_low = split(moments)
        member = onehot(iota((n_cells, chunk), 0) == map_ref[:, part])
        ratio[...] += mm(m_high, member, NT) + mm(m_low, member, NT)
        return carry

    lax.fori_loop(0, n_les // chunk, les_part, 0)
    ratio[:n_bins, :] = ratio[n_bins:, :] / jnp.maximum(ratio[:n_bins, :], floor_mass)

    each(lambda r: info_copy(r).wait_recv())
    for d in range(n):
        info_rows[d:d + 1, :] = info_in[d]
    table = info_rows[...].astype(bf16)
    spread = onehot(iota((slots, n), 0) // capp == iota((slots, n), 1))
    wide = mm(spread, table, NN)
    slot_in = lax.rem(iota((slots, 128), 0), capp)
    lanes = iota((slots, 128), 1)
    index_col = jnp.sum(jnp.where(lanes == slot_in, wide, 0.0), axis=1, keepdims=True)
    steps_col = jnp.sum(jnp.where(lanes == slot_in + 64, wide, 0.0), axis=1, keepdims=True)
    placed = index_col.astype(jnp.int32) == iota((slots, n_cells), 1) + 1
    unpack[...] = onehot(placed)
    step_row[...] = jnp.sum(jnp.where(placed, steps_col, 0.0), axis=0, keepdims=True)
    counts = jnp.zeros((n_cells + 4 * rim, n_cells), f32)
    entry = iota((n_cells + 4 * rim, n_cells), 0)
    for face in range(4):
        counts = counts + jnp.where(adj_ref[face:face + 1, :] == entry, 1.0, 0.0)
    counts = counts.astype(bf16)

    each(lambda r: state_copy(r).wait_recv())
    g_high, g_low = split(recv[...])
    rim_pick = unpack[:, :128]
    halo_out[...] = (mm(rim_pick, g_high, TN) + mm(rim_pick, g_low, TN))[:rim]

    beside = (
        (gx < n_gx - 1, (gx + 1, yz), 0, gx > 0),
        (gx > 0, (gx - 1, yz), 1, gx < n_gx - 1),
        (yz < n_yz - 1, (gx, yz + 1), 2, yz > 0),
        (yz > 0, (gx, yz - 1), 3, yz < n_yz - 1),
    )

    def halo_copy(dev, place):
        return pltpu.make_async_remote_copy(
            halo_out, halo_in.at[pl.ds(place * rim, rim)], h_send.at[place], h_recv.at[place],
            device_id=dev, device_id_type=pl.DeviceIdType.MESH)

    for there, dev, place, _ in beside:
        @pl.when(there)
        def _start():
            halo_copy(dev, place).start()

    home_state = mm(g_high, unpack[...], TN) + mm(g_low, unpack[...], TN)
    o_high, o_low = split(home_state)
    own_counts = counts[:n_cells]
    moved = home_state * (1.0 - 4.0 * tau_face) + tau_face * (
        mm(o_high, own_counts, NN) + mm(o_low, own_counts, NN))
    for _, dev, place, from_there in beside:
        @pl.when(from_there)
        def _wait():
            halo_copy(dev, place).wait_recv()
    r_high, r_low = split(halo_in[...])
    far_counts = counts[n_cells:]
    moved = moved + tau_face * (mm(r_high, far_counts, TN) + mm(r_low, far_counts, TN))
    q0[...] = moved.reshape(n_scalar, n_bins, n_cells)

    count = step_row[...]
    size = 1.0 / jnp.maximum(count, 1.0)
    bins_at = iota((n_bins, n_cells), 0)
    first, last = bins_at == 0, bins_at == n_bins - 1

    def substep(src, dst, s):
        h = jnp.where(s.astype(f32) < count, size, 0.0)
        rate = ratio[:n_bins, :] * h
        for j in range(n_scalar):
            mixed = coup_ref[j, 0] * src[0]
            for k in range(1, n_scalar):
                mixed = mixed + coup_ref[j, k] * src[k]
            q = src[j]
            below = jnp.where(first, q, pltpu.roll(q, 1, 0))
            above = jnp.where(last, q, pltpu.roll(q, n_bins - 1, 0))
            dst[j] = q + rate * (above - 2.0 * q + below) + h * jnp.tanh(mixed)

    def pair(i, carry):
        substep(q0, q1, 2 * i)
        substep(q1, q0, 2 * i + 1)
        return carry

    lax.fori_loop(0, submax // 2, pair, 0)

    n_high, n_low = split(q0[...].reshape(rows, n_cells))
    new_high[...] = n_high
    new_low[...] = n_low
    reply[...] = mm(unpack[...], n_high, NT) + mm(unpack[...], n_low, NT)
    each(lambda r: back_copy(r).start())
    back[mine, :] = reply[mine, :]

    def species_part(i, carry):
        part = pl.ds(pl.multiple_of(i * chunk, chunk), chunk)
        member = onehot(iota((n_cells, chunk), 0) == map_ref[:, part])
        w = weights[:, part]
        picked = mm(new_high[...], member, NN) + mm(new_low[...], member, NN)
        for k in range(n_scalar):
            species_ref[k:k + 1, part] = jnp.sum(
                picked[k * n_bins:(k + 1) * n_bins] * w, axis=0, keepdims=True)
        return carry

    lax.fori_loop(0, n_les // chunk, species_part, 0)

    each(lambda r: back_copy(r).wait_recv())
    b_high, b_low = split(back[...])
    cond_ref[...] = (mm(b_high, pack[...], TN) + mm(b_low, pack[...], TN)).reshape(
        n_scalar, n_bins, n_cells)

    def drain(r):
        info_copy(r).wait_send()
        state_copy(r).wait_send()
        back_copy(r).wait_send()

    each(drain)
    for there, dev, place, _ in beside:
        @pl.when(there)
        def _drain():
            halo_copy(dev, place).wait_send()


def shards(n_gx, n_yz, mean_mix, segregation, dissipation, les_map, cond_state, slot_cell,
           adjacency, substeps, coupling):
    n_scalar, n_bins, n_cells = cond_state.shape
    n_les = mean_mix.shape[0]
    n = n_gx * n_yz
    rows = n_scalar * n_bins
    cap = 2 * n_cells // n
    capp = -(-cap // 8) * 8
    slots = n * capp
    rim = n_cells // 8
    chunk = min(512, n_les)
    vmem = pl.BlockSpec(memory_space=pltpu.VMEM)
    dma = pltpu.SemaphoreType.DMA
    return pl.pallas_call(
        functools.partial(kernel, n_gx, n_yz, cap, chunk),
        out_shape=(
            jax.ShapeDtypeStruct((n_scalar, n_les), f32),
            jax.ShapeDtypeStruct((n_scalar, n_bins, n_cells), f32),
        ),
        in_specs=[vmem] * 8 + [pl.BlockSpec(memory_space=pltpu.SMEM)],
        out_specs=(vmem, vmem),
        scratch_shapes=[
            pltpu.VMEM((slots, rows), f32),
            pltpu.VMEM((slots, rows), f32),
            pltpu.VMEM((slots, rows), f32),
            pltpu.VMEM((slots, rows), f32),
            pltpu.VMEM((n, 1, 128), f32),
            pltpu.VMEM((n, 1, 128), f32),
            pltpu.VMEM((n, 128), f32),
            pltpu.VMEM((rim, rows), f32),
            pltpu.VMEM((4 * rim, rows), f32),
            pltpu.VMEM((n_bins, n_les), f32),
            pltpu.VMEM((2 * n_bins, n_cells), f32),
            pltpu.VMEM((slots, n_cells), bf16),
            pltpu.VMEM((slots, n_cells), bf16),
            pltpu.VMEM((n_scalar, n_bins, n_cells), f32),
            pltpu.VMEM((n_scalar, n_bins, n_cells), f32),
            pltpu.VMEM((rows, n_cells), bf16),
            pltpu.VMEM((rows, n_cells), bf16),
            pltpu.VMEM((1, n_cells), f32),
            dma((n,)), dma((n,)), dma((n,)), dma((n,)), dma((n,)), dma((n,)), dma((4,)), dma((4,)),
        ],
        compiler_params=pltpu.CompilerParams(
            collective_id=0, has_side_effects=True, vmem_limit_bytes=48 * 1024 * 1024),
        cost_estimate=pl.CostEstimate(
            flops=8 * rows * n_les * n_cells, bytes_accessed=4 * rows * n_cells,
            transcendentals=n_bins * n_les),
    )(
        mean_mix.reshape(1, n_les), segregation.reshape(1, n_les), dissipation.reshape(1, n_les),
        les_map.reshape(1, n_les), cond_state, slot_cell.reshape(1, n_cells), adjacency,
        substeps.reshape(1, n_cells), coupling,
    )


def solution(mesh):
    both = P(("gx", "yz"))
    placed = (both, both, both, both, P(None, None, ("gx", "yz")), both,
              P(None, ("gx", "yz")), both, P())
    return jax.shard_map(
        functools.partial(shards, mesh.shape["gx"], mesh.shape["yz"]),
        mesh=mesh,
        in_specs=placed,
        out_specs=(P(None, ("gx", "yz")), P(None, None, ("gx", "yz"))),
        check_vma=False,
    )
```

time: 260 us -> 91.9 us (0.35)
  the two profiles are of different devices: /device:TPU:0 before, /device:TPU:31 now
where the time goes in v1:
time: 91.9 us; the launch traced here: 91.3 us
  Pallas kernels  83.8 us (91%)
  local copies, waits for them, and re-layouts  6.87 us (7%)
    pallas_call x1, Pallas kernels, shards(): pl.pallas_call(functools.partial(kernel, n_gx, n_yz, cap, chunk), out_sha...  83.8 us
    unnamed x20, local copies, waits for them, and re-layouts  6.87 us

profile of v1, /device:TPU:31, one launch (start us, length us, event | category | flops | bytes accessed | tf_op | source)
XLA Modules:
  0.0 91.3 jit_solution(17291596170820186219)
XLA Ops:
  0.6 0.0 copy-start.5
  0.6 0.0 copy-start.8
  0.7 0.0 copy-start.7
  0.7 0.7 copy-done.5
  1.3 0.0 copy-done.8
  1.3 0.0 copy-done.7
  1.3 0.0 copy-start
  1.3 1.1 %copy-done = f32[10,64,256]{2,1,0:T(8,128)S(1)} copy-done((f32[10,64,256]{2,1,0:T(8,128)S(1)}, f32[10,64,256]{2,1,0:T(8,128)}, u32[]{:S(2)}) %copy-start) | copy-done | bytes 655384
  2.4 0.0 copy-start.1
  2.4 0.7 copy-done.1
  3.2 0.0 copy-start.2
  3.2 0.7 copy-done.2
  3.9 0.0 copy-start.3
  3.9 0.7 copy-done.3
  4.6 0.0 copy-start.4
  4.6 0.7 copy-done.4
  5.3 0.0 copy-start.6
  5.3 0.7 copy-done.6
  6.0 83.8 %shard_map.104 = (f32[10,4096]{1,0:T(8,128)S(1)}, f32[10,64,256]{2,1,0:T(8,128)S(1)}) custom-call(f32[1,4096]{1,0:T(1,128)S(1)} %bitcast.6, f32[1,4096]{1,0:T(1,128)S(1)} %bitcast.7, f32[1,4096]{1,0:T(1,128)S(1)} %bitcast.8, s32[1,4096]{1,0:T(1,128)S(1)} %bitcast.9, f32[10,64,256]{2,1,0:T(8,128)S(1)} %copy-done, s32[1,256]{1,0:T(1,128)S(1)} %bitcast.10, ...), custom_call_target="tpu_custom_call" | custom-call | flops 5368709120 | bytes 655360 | tf_op jit(solution)/shard_map/pallas_call | solution.py:276
  89.7 0.7 copy.13
  90.5 0.8 copy.14
Async XLA Ops:
  0.6 0.7 copy-start.5
  0.6 0.7 copy-start.8
  0.7 0.7 copy-start.7
  1.3 1.1 %copy-start = (f32[10,64,256]{2,1,0:T(8,128)S(1)}, f32[10,64,256]{2,1,0:T(8,128)}, u32[]{:S(2)}) copy-start(f32[10,64,256]{2,1,0:T(8,128)} %state_ref.1) | copy-start | bytes 1966084
  2.4 0.7 copy-start.1
  3.2 0.7 copy-start.2
  3.9 0.7 copy-start.3
  4.6 0.7 copy-start.4
  5.3 0.7 copy-start.6

commit v2 on v1

--- a/solution.py
+++ b/solution.py
@@ -36,11 +36,12 @@
 
 def kernel(
     n_gx, n_yz, cap, chunk,
+    mean_hbm, seg_hbm, diss_hbm, map_hbm, state_hbm, slot_hbm, adj_hbm, steps_hbm, coup_hbm,
+    species_ref, cond_ref,
     mean_ref, seg_ref, diss_ref, map_ref, state_ref, slot_ref, adj_ref, steps_ref, coup_ref,
-    species_ref, cond_ref,
     send, recv, reply, back, info_out, info_in, info_rows, halo_out, halo_in,
-    weights, ratio, pack, unpack, q0, q1, new_high, new_low, step_row,
-    s_send, s_recv, i_send, i_recv, b_send, b_recv, h_send, h_recv,
+    weights, ratio, pack, unpack, q0, q1, new_high, new_low, step_row, rim_sum,
+    a_sem,    s_send, s_recv, i_send, i_recv, b_send, b_recv, h_send, h_recv,
 ):
     n_scalar, n_bins, n_cells = state_ref.shape
     rows = n_scalar * n_bins
@@ -50,51 +51,83 @@
     capp = slots // n
     rim = halo_out.shape[0]
     gx, yz = lax.axis_index("gx"), lax.axis_index("yz")
-    me = gx * n_yz + yz
-
-    def coords(r):
-        t = lax.rem(me + r, n)
-        return t, (t // n_yz, lax.rem(t, n_yz))
-
-    def block(ref, t):
-        return ref.at[pl.ds(pl.multiple_of(t * capp, 8), capp)]
-
-    def info_copy(r):
-        t, dev = coords(r)
+    mesh_id = pl.DeviceIdType.MESH
+    half = n_gx // 2
+    groups = 4
+    per = n // groups
+    width = slots // groups
+
+    def steps_of(b):
+        i = b // n_yz
+        odd = lax.rem(i, 2)
+        dg = lax.rem(half + (1 - 2 * odd) * ((i + 1) // 2) + n_gx, n_gx)
+        return dg, n_yz - 1 - lax.rem(b, n_yz)
+
+    def ahead(b):
+        dg, dy = steps_of(b)
+        return lax.rem(gx + dg, n_gx), lax.rem(yz + dy, n_yz)
+
+    def behind(b):
+        dg, dy = steps_of(b)
+        return lax.rem(gx - dg + n_gx, n_gx), lax.rem(yz - dy + n_yz, n_yz)
+
+    def block(ref, b):
+        return ref.at[pl.ds(pl.multiple_of(b * capp, 8), capp)]
+
+    def info_copy(b):
         return pltpu.make_async_remote_copy(
-            info_out.at[t], info_in.at[me], i_send.at[r], i_recv.at[r],
-            device_id=dev, device_id_type=pl.DeviceIdType.MESH)
-
-    def state_copy(r):
-        t, dev = coords(r)
+            info_out.at[b], info_in.at[b], i_send.at[b], i_recv.at[b],
+            device_id=ahead(b), device_id_type=mesh_id)
+
+    def state_copy(b):
         return pltpu.make_async_remote_copy(
-            block(send, t), block(recv, me), s_send.at[r], s_recv.at[r],
-            device_id=dev, device_id_type=pl.DeviceIdType.MESH)
-
-    def back_copy(r):
-        t, dev = coords(r)
+            block(send, b), block(recv, b), s_send.at[b], s_recv.at[b],
+            device_id=ahead(b), device_id_type=mesh_id)
+
+    def back_copy(b):
         return pltpu.make_async_remote_copy(
-            block(reply, t), block(back, me), b_send.at[r], b_recv.at[r],
-            device_id=dev, device_id_type=pl.DeviceIdType.MESH)
-
-    def each(body):
-        def run(r, carry):
-            body(r)
+            block(reply, b), block(back, b), b_send.at[b], b_recv.at[b],
+            device_id=behind(b), device_id_type=mesh_id)
+
+    def each(body, low=0, high=n - 1):
+        def run(b, carry):
+            body(b)
             return carry
-        lax.fori_loop(1, n, run, 0)
+        lax.fori_loop(low, high, run, 0)
+
+    def each_of(group, body):
+        each(body, group * per, min((group + 1) * per, n - 1))
+
+    def rows_of(group):
+        return pl.ds(group * width, width)
+
+    fetches = [
+        pltpu.make_async_copy(src, dst, a_sem.at[i])
+        for i, (src, dst) in enumerate((
+            (slot_hbm, slot_ref), (steps_hbm, steps_ref), (state_hbm, state_ref),
+            (mean_hbm, mean_ref), (seg_hbm, seg_ref), (diss_hbm, diss_ref),
+            (map_hbm, map_ref), (adj_hbm, adj_ref), (coup_hbm, coup_ref)))
+    ]
+    for fetch in fetches:
+        fetch.start()
 
     halo_in[...] = jnp.zeros_like(halo_in)
     barrier = pltpu.get_barrier_semaphore()
 
-    def greet(r):
-        _, dev = coords(r)
-        pl.semaphore_signal(barrier, inc=1, device_id=dev, device_id_type=pl.DeviceIdType.MESH)
+    def greet(b):
+        pl.semaphore_signal(barrier, inc=1, device_id=ahead(b), device_id_type=mesh_id)
 
     each(greet)
 
+    fetches[0].wait()
+    fetches[1].wait()
     slot = slot_ref[...]
-    home = slot // n_cells
-    local = slot - home * n_cells
+    tile = slot // n_cells
+    local = slot - tile * n_cells
+    tile_g = tile // n_yz
+    from_half = lax.rem(tile_g - gx + n_gx, n_gx) - half
+    step_i = jnp.where(from_half >= 0, 2 * from_half, -2 * from_half - 1)
+    home = step_i * n_yz + n_yz - 1 - lax.rem(tile - tile_g * n_yz - yz + n_yz, n_yz)
     marks = iota((n, n_cells), 0) == home
     before = onehot(iota((n_cells, n_cells), 0) < iota((n_cells, n_cells), 1))
     earlier = mm(onehot(marks), before, NN)
@@ -112,15 +145,21 @@
     for d in range(n):
         info_out[d] = info[d:d + 1, :]
 
+    fetches[2].wait()
     high, low = split(state_ref[...].reshape(rows, n_cells))
-    send[...] = mm(pack[...], high, NT) + mm(pack[...], low, NT)
-
+    send[rows_of(0), :] = mm(pack[rows_of(0), :], high, NT) + mm(pack[rows_of(0), :], low, NT)
     pl.semaphore_wait(barrier, n - 1)
-    each(lambda r: info_copy(r).start())
-    each(lambda r: state_copy(r).start())
-    info_in[pl.ds(me, 1)] = info_out[pl.ds(me, 1)]
-    mine = pl.ds(pl.multiple_of(me * capp, 8), capp)
+    each(lambda b: info_copy(b).start())
+    each_of(0, lambda b: state_copy(b).start())
+    for g in range(1, groups):
+        part = rows_of(g)
+        send[part, :] = mm(pack[part, :], high, NT) + mm(pack[part, :], low, NT)
+        each_of(g, lambda b: state_copy(b).start())
+    info_in[n - 1] = info_out[n - 1]
+    mine = pl.ds(slots - capp, capp)
     recv[mine, :] = send[mine, :]
+    for fetch in fetches[3:]:
+        fetch.wait()
 
     centre = (iota((n_bins, 128), 0).astype(f32) + 0.5) / n_bins
     log_low = jnp.log(centre)[:, :1]
@@ -145,7 +184,7 @@
     lax.fori_loop(0, n_les // chunk, les_part, 0)
     ratio[:n_bins, :] = ratio[n_bins:, :] / jnp.maximum(ratio[:n_bins, :], floor_mass)
 
-    each(lambda r: info_copy(r).wait_recv())
+    each(lambda b: info_copy(b).wait_recv())
     for d in range(n):
         info_rows[d:d + 1, :] = info_in[d]
     table = info_rows[...].astype(bf16)
@@ -164,10 +203,23 @@
         counts = counts + jnp.where(adj_ref[face:face + 1, :] == entry, 1.0, 0.0)
     counts = counts.astype(bf16)
 
-    each(lambda r: state_copy(r).wait_recv())
-    g_high, g_low = split(recv[...])
-    rim_pick = unpack[:, :128]
-    halo_out[...] = (mm(rim_pick, g_high, TN) + mm(rim_pick, g_low, TN))[:rim]
+    for g in range(groups):
+        part = rows_of(g)
+        each_of(g, lambda b: state_copy(b).wait_recv())
+        g_high, g_low = split(recv[part, :])
+        into = unpack[part, :]
+        more = mm(g_high, into, TN) + mm(g_low, into, TN)
+        rim_more = mm(into[:, :128], g_high, TN) + mm(into[:, :128], g_low, TN)
+        more = more.reshape(n_scalar, n_bins, n_cells)
+        if g == 0:
+            q1[...] = more
+            rim_sum[...] = rim_more
+        elif g < groups - 1:
+            q1[...] += more
+            rim_sum[...] += rim_more
+        else:
+            halo_out[...] = (rim_sum[...] + rim_more)[:rim]
+            q1[...] += more
 
     beside = (
         (gx < n_gx - 1, (gx + 1, yz), 0, gx > 0),
@@ -179,14 +231,14 @@
     def halo_copy(dev, place):
         return pltpu.make_async_remote_copy(
             halo_out, halo_in.at[pl.ds(place * rim, rim)], h_send.at[place], h_recv.at[place],
-            device_id=dev, device_id_type=pl.DeviceIdType.MESH)
+            device_id=dev, device_id_type=mesh_id)
 
     for there, dev, place, _ in beside:
         @pl.when(there)
         def _start():
             halo_copy(dev, place).start()
 
-    home_state = mm(g_high, unpack[...], TN) + mm(g_low, unpack[...], TN)
+    home_state = q1[...].reshape(rows, n_cells)
     o_high, o_low = split(home_state)
     own_counts = counts[:n_cells]
     moved = home_state * (1.0 - 4.0 * tau_face) + tau_face * (
@@ -227,8 +279,10 @@
     n_high, n_low = split(q0[...].reshape(rows, n_cells))
     new_high[...] = n_high
     new_low[...] = n_low
-    reply[...] = mm(unpack[...], n_high, NT) + mm(unpack[...], n_low, NT)
-    each(lambda r: back_copy(r).start())
+    for g in range(groups):
+        part = rows_of(g)
+        reply[part, :] = mm(unpack[part, :], n_high, NT) + mm(unpack[part, :], n_low, NT)
+        each_of(g, lambda b: back_copy(b).start())
     back[mine, :] = reply[mine, :]
 
     def species_part(i, carry):
@@ -243,10 +297,16 @@
 
     lax.fori_loop(0, n_les // chunk, species_part, 0)
 
-    each(lambda r: back_copy(r).wait_recv())
-    b_high, b_low = split(back[...])
-    cond_ref[...] = (mm(b_high, pack[...], TN) + mm(b_low, pack[...], TN)).reshape(
-        n_scalar, n_bins, n_cells)
+    for g in range(groups):
+        part = rows_of(g)
+        each_of(g, lambda b: back_copy(b).wait_recv())
+        b_high, b_low = split(back[part, :])
+        more = (mm(b_high, pack[part, :], TN) + mm(b_low, pack[part, :], TN)).reshape(
+            n_scalar, n_bins, n_cells)
+        if g == 0:
+            cond_ref[...] = more
+        else:
+            cond_ref[...] += more
 
     def drain(r):
         info_copy(r).wait_send()
@@ -279,9 +339,18 @@
             jax.ShapeDtypeStruct((n_scalar, n_les), f32),
             jax.ShapeDtypeStruct((n_scalar, n_bins, n_cells), f32),
         ),
-        in_specs=[vmem] * 8 + [pl.BlockSpec(memory_space=pltpu.SMEM)],
+        in_specs=[pl.BlockSpec(memory_space=pltpu.HBM)] * 9,
         out_specs=(vmem, vmem),
         scratch_shapes=[
+            pltpu.VMEM((1, n_les), f32),
+            pltpu.VMEM((1, n_les), f32),
+            pltpu.VMEM((1, n_les), f32),
+            pltpu.VMEM((1, n_les), jnp.int32),
+            pltpu.VMEM((n_scalar, n_bins, n_cells), f32),
+            pltpu.VMEM((1, n_cells), jnp.int32),
+            pltpu.VMEM((4, n_cells), jnp.int32),
+            pltpu.VMEM((1, n_cells), jnp.int32),
+            pltpu.SMEM(coupling.shape, f32),
             pltpu.VMEM((slots, rows), f32),
             pltpu.VMEM((slots, rows), f32),
             pltpu.VMEM((slots, rows), f32),
@@ -300,7 +369,8 @@
             pltpu.VMEM((rows, n_cells), bf16),
             pltpu.VMEM((rows, n_cells), bf16),
             pltpu.VMEM((1, n_cells), f32),
-            dma((n,)), dma((n,)), dma((n,)), dma((n,)), dma((n,)), dma((n,)), dma((4,)), dma((4,)),
+            pltpu.VMEM((128, rows), f32),
+            dma((9,)), dma((n,)), dma((n,)), dma((n,)), dma((n,)), dma((n,)), dma((n,)), dma((4,)), dma((4,)),
         ],
         compiler_params=pltpu.CompilerParams(
             collective_id=0, has_side_effects=True, vmem_limit_bytes=48 * 1024 * 1024),

time: 91.9 us -> 86.8 us (0.945)
  the two profiles are of different devices: /device:TPU:31 before, /device:TPU:0 now
where the time goes in v2:
time: 86.8 us; the launch traced here: 85.2 us
  Pallas kernels  77.6 us (89%)
  local copies, waits for them, and re-layouts  6.87 us (8%)
    pallas_call x1, Pallas kernels, shards(): pl.pallas_call(functools.partial(kernel, n_gx, n_yz, cap, chunk), out_sha...  77.6 us
    unnamed x20, local copies, waits for them, and re-layouts  6.87 us

profile of v2, /device:TPU:0, one launch (start us, length us, event | category | flops | bytes accessed | tf_op | source)
XLA Modules:
  0.0 85.2 jit_solution(13789960346813818017)
XLA Ops:
  0.6 0.0 copy-start.5
  0.6 0.0 copy-start.8
  0.7 0.0 copy-start.7
  0.7 0.7 copy-done.5
  1.3 0.0 copy-done.8
  1.3 0.0 copy-done.7
  1.3 0.0 copy-start
  1.3 1.1 %copy-done = f32[10,64,256]{2,1,0:T(8,128)S(1)} copy-done((f32[10,64,256]{2,1,0:T(8,128)S(1)}, f32[10,64,256]{2,1,0:T(8,128)}, u32[]{:S(2)}) %copy-start) | copy-done | bytes 655384
  2.4 0.0 copy-start.1
  2.4 0.7 copy-done.1
  3.2 0.0 copy-start.2
  3.2 0.7 copy-done.2
  3.9 0.0 copy-start.3
  3.9 0.7 copy-done.3
  4.6 0.0 copy-start.4
  4.6 0.7 copy-done.4
  5.3 0.0 copy-start.6
  5.3 0.7 copy-done.6
  6.0 77.6 %shard_map.104 = (f32[10,4096]{1,0:T(8,128)S(1)}, f32[10,64,256]{2,1,0:T(8,128)S(1)}) custom-call(f32[1,4096]{1,0:T(1,128)S(1)} %bitcast.6, f32[1,4096]{1,0:T(1,128)S(1)} %bitcast.7, f32[1,4096]{1,0:T(1,128)S(1)} %bitcast.8, s32[1,4096]{1,0:T(1,128)S(1)} %bitcast.9, f32[10,64,256]{2,1,0:T(8,128)S(1)} %copy-done, s32[1,256]{1,0:T(1,128)S(1)} %bitcast.10, ...), custom_call_target="tpu_custom_call" | custom-call | flops 5368709120 | bytes 655360 | tf_op jit(solution)/shard_map/pallas_call | solution.py:336
  83.6 0.7 copy.13
  84.3 0.8 copy.14
Async XLA Ops:
  0.6 0.7 copy-start.5
  0.6 0.7 copy-start.8
  0.7 0.7 copy-start.7
  1.3 1.1 %copy-start = (f32[10,64,256]{2,1,0:T(8,128)S(1)}, f32[10,64,256]{2,1,0:T(8,128)}, u32[]{:S(2)}) copy-start(f32[10,64,256]{2,1,0:T(8,128)} %state_hbm.1) | copy-start | bytes 1966084
  2.4 0.7 copy-start.1
  3.2 0.7 copy-start.2
  3.9 0.7 copy-start.3
  4.6 0.7 copy-start.4
  5.3 0.7 copy-start.6

commit v3 on v2

--- a/solution.py
+++ b/solution.py
@@ -54,49 +54,60 @@
     mesh_id = pl.DeviceIdType.MESH
     half = n_gx // 2
     groups = 4
-    per = n // groups
     width = slots // groups
 
-    def steps_of(b):
-        i = b // n_yz
-        odd = lax.rem(i, 2)
-        dg = lax.rem(half + (1 - 2 * odd) * ((i + 1) // 2) + n_gx, n_gx)
-        return dg, n_yz - 1 - lax.rem(b, n_yz)
+    def wrap(a, size):
+        a = jnp.where(a >= size, a - size, a)
+        return jnp.where(a < 0, a + size, a)
+
+    def dg_of(i):
+        odd = i - 2 * (i // 2)
+        return half + (1 - 2 * odd) * ((i + 1) // 2)
 
     def ahead(b):
-        dg, dy = steps_of(b)
-        return lax.rem(gx + dg, n_gx), lax.rem(yz + dy, n_yz)
+        i, j = b
+        return wrap(gx + dg_of(i), n_gx), wrap(yz + (n_yz - 1 - j), n_yz)
 
     def behind(b):
-        dg, dy = steps_of(b)
-        return lax.rem(gx - dg + n_gx, n_gx), lax.rem(yz - dy + n_yz, n_yz)
+        i, j = b
+        return wrap(gx - dg_of(i), n_gx), wrap(yz - (n_yz - 1 - j), n_yz)
+
+    def number(b):
+        return b[0] * n_yz + b[1]
 
     def block(ref, b):
-        return ref.at[pl.ds(pl.multiple_of(b * capp, 8), capp)]
+        return ref.at[pl.ds(pl.multiple_of(number(b) * capp, 8), capp)]
 
     def info_copy(b):
+        m = number(b)
         return pltpu.make_async_remote_copy(
-            info_out.at[b], info_in.at[b], i_send.at[b], i_recv.at[b],
+            info_out.at[m], info_in.at[m], i_send.at[m], i_recv.at[m],
             device_id=ahead(b), device_id_type=mesh_id)
 
     def state_copy(b):
+        m = number(b)
         return pltpu.make_async_remote_copy(
-            block(send, b), block(recv, b), s_send.at[b], s_recv.at[b],
+            block(send, b), block(recv, b), s_send.at[m], s_recv.at[m],
             device_id=ahead(b), device_id_type=mesh_id)
 
     def back_copy(b):
+        m = number(b)
         return pltpu.make_async_remote_copy(
-            block(reply, b), block(back, b), b_send.at[b], b_recv.at[b],
+            block(reply, b), block(back, b), b_send.at[m], b_recv.at[m],
             device_id=behind(b), device_id_type=mesh_id)
 
-    def each(body, low=0, high=n - 1):
-        def run(b, carry):
-            body(b)
+    def each(body, low=0, high=n_gx):
+        def run(i, carry):
+            for j in range(n_yz):
+                body((i, j))
             return carry
-        lax.fori_loop(low, high, run, 0)
+        lax.fori_loop(low, min(high, n_gx - 1), run, 0)
+        if high == n_gx:
+            for j in range(n_yz - 1):
+                body((n_gx - 1, j))
 
     def each_of(group, body):
-        each(body, group * per, min((group + 1) * per, n - 1))
+        each(body, group * (n_gx // groups), (group + 1) * (n_gx // groups))
 
     def rows_of(group):
         return pl.ds(group * width, width)
@@ -297,8 +308,19 @@
 
     lax.fori_loop(0, n_les // chunk, species_part, 0)
 
+    def drain(b):
+        info_copy(b).wait_send()
+        state_copy(b).wait_send()
+
+    each(drain)
+    for there, dev, place, _ in beside:
+        @pl.when(there)
+        def _drain():
+            halo_copy(dev, place).wait_send()
+
     for g in range(groups):
         part = rows_of(g)
+        each_of(g, lambda b: back_copy(b).wait_send())
         each_of(g, lambda b: back_copy(b).wait_recv())
         b_high, b_low = split(back[part, :])
         more = (mm(b_high, pack[part, :], TN) + mm(b_low, pack[part, :], TN)).reshape(
@@ -307,17 +329,6 @@
             cond_ref[...] = more
         else:
             cond_ref[...] += more
-
-    def drain(r):
-        info_copy(r).wait_send()
-        state_copy(r).wait_send()
-        back_copy(r).wait_send()
-
-    each(drain)
-    for there, dev, place, _ in beside:
-        @pl.when(there)
-        def _drain():
-            halo_copy(dev, place).wait_send()
 
 
 def shards(n_gx, n_yz, mean_mix, segregation, dissipation, les_map, cond_state, slot_cell,
@@ -373,7 +384,7 @@
             dma((9,)), dma((n,)), dma((n,)), dma((n,)), dma((n,)), dma((n,)), dma((n,)), dma((4,)), dma((4,)),
         ],
         compiler_params=pltpu.CompilerParams(
-            collective_id=0, has_side_effects=True, vmem_limit_bytes=48 * 1024 * 1024),
+            collective_id=0, has_side_effects=True, vmem_limit_bytes=64 * 1024 * 1024),
         cost_estimate=pl.CostEstimate(
             flops=8 * rows * n_les * n_cells, bytes_accessed=4 * rows * n_cells,
             transcendentals=n_bins * n_les),

time: 86.8 us -> 82.9 us (0.955)
  local copies, waits for them, and re-layouts: 6.87 us -> 3.64 us
    unnamed x20 -> x2, local copies, waits for them, and re-layouts: 6.87 us -> 3.64 us
where the time goes in v3:
time: 82.9 us; the launch traced here: 81.9 us
  Pallas kernels  77.6 us (94%)
  local copies, waits for them, and re-layouts  3.64 us (4%)
    pallas_call x1, Pallas kernels, shards(): pl.pallas_call(functools.partial(kernel, n_gx, n_yz, cap, chunk), out_sha...  77.6 us
    unnamed x2, local copies, waits for them, and re-layouts  3.64 us

profile of v3, /device:TPU:0, one launch (start us, length us, event | category | flops | bytes accessed | tf_op | source)
XLA Modules:
  0.0 81.9 jit_solution(17406343724957301986)
XLA Ops:
  0.6 77.6 %shard_map.104 = (f32[10,4096]{1,0:T(8,128)}, f32[10,64,256]{2,1,0:T(8,128)}) custom-call(f32[1,4096]{1,0:T(1,128)} %bitcast.6, f32[1,4096]{1,0:T(1,128)} %bitcast.7, f32[1,4096]{1,0:T(1,128)} %bitcast.8, s32[1,4096]{1,0:T(1,128)} %bitcast.9, f32[10,64,256]{2,1,0:T(8,128)} %state_hbm.1, s32[1,256]{1,0:T(1,128)} %bitcast.10, s32[4,256]{1,0:T(4,128)} %adj_hbm.1, ...), custom_call_target="tpu_custom_call" | custom-call | flops 5368709120 | bytes 655360 | tf_op jit(solution)/shard_map/pallas_call | solution.py:347
  78.2 1.7 %copy.13 = f32[10,4096]{1,0:T(8,128)} copy(f32[10,4096]{1,0:T(8,128)} %get-tuple-element.4) | data formatting | bytes 327680
  79.9 2.0 %copy.14 = f32[10,64,256]{2,1,0:T(8,128)} copy(f32[10,64,256]{2,1,0:T(8,128)} %get-tuple-element.5) | data formatting | bytes 1310720

commit v4 on v3

--- a/solution.py
+++ b/solution.py
@@ -53,7 +53,7 @@
     gx, yz = lax.axis_index("gx"), lax.axis_index("yz")
     mesh_id = pl.DeviceIdType.MESH
     half = n_gx // 2
-    groups = 4
+    groups = n_gx
     width = slots // groups
 
     def wrap(a, size):
@@ -160,8 +160,8 @@
     high, low = split(state_ref[...].reshape(rows, n_cells))
     send[rows_of(0), :] = mm(pack[rows_of(0), :], high, NT) + mm(pack[rows_of(0), :], low, NT)
     pl.semaphore_wait(barrier, n - 1)
+    each_of(0, lambda b: state_copy(b).start())
     each(lambda b: info_copy(b).start())
-    each_of(0, lambda b: state_copy(b).start())
     for g in range(1, groups):
         part = rows_of(g)
         send[part, :] = mm(pack[part, :], high, NT) + mm(pack[part, :], low, NT)

time: 82.9 us -> 84.3 us (1.017)
  Pallas kernels: 77.6 us -> 79.8 us
    pallas_call x1, Pallas kernels: 77.6 us -> 79.8 us  [shards(): pl.pallas_call(functools.partial(kernel, n_gx, n_yz, cap, chunk), out_sha...]
where the time goes in v4:
time: 84.3 us; the launch traced here: 84.1 us
  Pallas kernels  79.8 us (95%)
  local copies, waits for them, and re-layouts  3.64 us (4%)
    pallas_call x1, Pallas kernels, shards(): pl.pallas_call(functools.partial(kernel, n_gx, n_yz, cap, chunk), out_sha...  79.8 us
    unnamed x2, local copies, waits for them, and re-layouts  3.64 us

profile of v4, /device:TPU:0, one launch (start us, length us, event | category | flops | bytes accessed | tf_op | source)
XLA Modules:
  0.0 84.1 jit_solution(10584999400348700852)
XLA Ops:
  0.6 79.8 %shard_map.104 = (f32[10,4096]{1,0:T(8,128)}, f32[10,64,256]{2,1,0:T(8,128)}) custom-call(f32[1,4096]{1,0:T(1,128)} %bitcast.6, f32[1,4096]{1,0:T(1,128)} %bitcast.7, f32[1,4096]{1,0:T(1,128)} %bitcast.8, s32[1,4096]{1,0:T(1,128)} %bitcast.9, f32[10,64,256]{2,1,0:T(8,128)} %state_hbm.1, s32[1,256]{1,0:T(1,128)} %bitcast.10, s32[4,256]{1,0:T(4,128)} %adj_hbm.1, ...), custom_call_target="tpu_custom_call" | custom-call | flops 5368709120 | bytes 655360 | tf_op jit(solution)/shard_map/pallas_call | solution.py:347
  80.4 1.7 %copy.13 = f32[10,4096]{1,0:T(8,128)} copy(f32[10,4096]{1,0:T(8,128)} %get-tuple-element.4) | data formatting | bytes 327680
  82.1 2.0 %copy.14 = f32[10,64,256]{2,1,0:T(8,128)} copy(f32[10,64,256]{2,1,0:T(8,128)} %get-tuple-element.5) | data formatting | bytes 1310720
